TPU v7x, 512 devices: a whole 4x8x8 slice. The times are simulated.
512 devices in a mesh: dp: 128 (over x_hi, z, y), group: 4 (over x_lo, core).
Axes of the slice: x: 4 (x_hi: 2, x_lo: 2; x = x_hi * 2 + x_lo), y: 8, z: 8, core: 2. Of those that a mesh axis runs over, the one named last changes fastest.
Arguments:
- image_embeds: bfloat16 [262144, 1152], P(('group', 'dp')), parts along dimension 0, may hold values from -0.1796875 to 0.1796875
- text_embeds: bfloat16 [262144, 1152], P(('group', 'dp')), parts along dimension 0, may hold values from -0.1796875 to 0.1796875
- logit_scale: float32 [1], replicated, may hold values from 4 to 16
- logit_bias: float32 [1], replicated, may hold values from -4 to -1
Outputs:
- image_grad: bfloat16 [262144, 1152], P(('group', 'dp')), parts along dimension 0
- text_grad: bfloat16 [262144, 1152], P(('group', 'dp')), parts along dimension 0
- image_loss: float32 [262144], P(('group', 'dp')), parts along dimension 0
There are 4 independent parts, one for each index of `group`. A program takes and returns all parts, laid end to end along the dimension named above; an argument that names none is the same for every part. Nothing has to cross between parts.
All inputs are finite; a program needn't handle non-finite values.
Results may differ from a plain program's by a relative error of at most 0.009.
Values may be sent and summed in bfloat16 or wider, within the bound.
A program may use at most 64 MiB of HBM per device.

v0:
```python
import jax
import jax.numpy as jnp
from jax import lax
from jax.sharding import PartitionSpec as P

STEPS = 4


EPS = 1e-06


def shifted(value, axis, steps):
    count = lax.axis_size(axis)
    pairs = [(source, (source + steps) % count) for source in range(count)]
    return lax.ppermute(value, axis, pairs)


def normalize(embeds):
    widened = embeds.astype(jnp.float32)
    inverse = lax.rsqrt(jnp.sum(widened * widened, axis=-1, keepdims=True) + EPS)
    return ((widened * inverse).astype(jnp.bfloat16), inverse)


def project_back(normed, inverse, upstream):
    widened = normed.astype(jnp.float32)
    along = jnp.sum(widened * upstream, axis=-1, keepdims=True)
    return ((upstream - widened * along) * inverse).astype(jnp.bfloat16)


def local(image_embeds, text_embeds, logit_scale, logit_bias):
    img_norm, img_inv = normalize(image_embeds)
    txt_norm, txt_inv = normalize(text_embeds)
    scale_value = logit_scale[0]
    bias_value = logit_bias[0]
    row_count = img_norm.shape[0]
    positions = jnp.arange(row_count)
    diagonal = (positions[:, None] == positions[None, :]).astype(jnp.float32)
    cycle_size = lax.axis_size("dp")
    image_acc = jnp.zeros(img_norm.shape, jnp.float32)
    loss_acc = jnp.zeros((row_count,), jnp.float32)
    text_block = txt_norm
    text_acc = jnp.zeros(img_norm.shape, jnp.float32)
    for offset in range(STEPS):
        if offset > 0:
            text_block = shifted(text_block, "dp", 1)
        labels = 2.0 * diagonal - 1.0 if offset == 0 else -jnp.ones_like(diagonal)
        similar = lax.dot_general(
            img_norm, text_block, (((1,), (1,)), ((), ())), preferred_element_type=jnp.float32
        )
        logits = scale_value * similar + bias_value
        loss_acc = loss_acc + jnp.sum(jax.nn.softplus(-labels * logits), axis=-1)
        logit_grad = -labels * jax.nn.sigmoid(-labels * logits)
        weights = (scale_value * logit_grad).astype(jnp.bfloat16)
        image_acc = image_acc + jnp.dot(weights, text_block, preferred_element_type=jnp.float32)
        partial_grad = lax.dot_general(
            weights, img_norm, (((0,), (0,)), ((), ())), preferred_element_type=jnp.float32
        )
        if offset == 0:
            text_acc = partial_grad
        else:
            text_acc = shifted(text_acc, "dp", 1) + partial_grad
    text_acc = shifted(text_acc, "dp", cycle_size - (STEPS - 1))
    image_grad = project_back(img_norm, img_inv, image_acc)
    text_grad = project_back(txt_norm, txt_inv, text_acc)
    image_loss = loss_acc / (STEPS * row_count)
    return (image_grad, text_grad, image_loss)


def solution(mesh):
    in_specs = (P(("group", "dp"), None), P(("group", "dp"), None), P(), P())
    out_specs = (P(("group", "dp"), None), P(("group", "dp"), None), P(("group", "dp")))
    return jax.shard_map(local, mesh=mesh, in_specs=in_specs, out_specs=out_specs, check_vma=False)
```

profile of v0, /device:TPU:1, one launch (start us, length us, event | category | flops | bytes accessed | tf_op | source)
XLA Modules:
  0.0 433.7 jit_solution(3164304541437367497)
XLA Ops:
  0.6 0.0 copy-start.1
  0.6 0.0 copy-start
  0.7 1.7 fusion
  2.4 1.6 fusion.2
  4.0 0.0 copy-done
  4.0 0.3 fusion.3
  5.6 0.0 copy-done.1
  5.6 1.5 fusion.17
  7.1 1.1 fusion.23
  8.2 4.0 collective-permute-start.3
  12.3 3.2 collective-permute-start
  15.5 85.9 %collective-permute-done = bf16[512,1152]{1,0:T(8,128)(2,1)S(1)} collective-permute-done((bf16[512,1152]{1,0:T(8,128)(2,1)S(1)}, bf16[512,1152]{1,0:T(8,128)(2,1)S(1)}, u32[]{:S(2)}, u32[]{:S(2)}) %collective-permute-start) | collective-permute-done | bytes 1179680 | tf_op jit(solution)/shard_map/ppermute | solution.py:15
  101.4 1.5 fusion.18
  102.9 0.0 collective-permute-done.3
  102.9 1.1 convolution_add_fusion
  103.9 1.9 collective-permute-start.4
  105.9 1.9 collective-permute-start.1
  107.8 80.6 %collective-permute-done.1 = bf16[512,1152]{1,0:T(8,128)(2,1)S(1)} collective-permute-done((bf16[512,1152]{1,0:T(8,128)(2,1)S(1)}, bf16[512,1152]{1,0:T(8,128)(2,1)S(1)}, u32[]{:S(2)}, u32[]{:S(2)}) %collective-permute-start.1) | collective-permute-done | bytes 1179680 | tf_op jit(solution)/shard_map/ppermute | solution.py:15
  188.4 1.5 fusion.19
  189.9 1.1 fusion.21
  191.0 0.0 collective-permute-done.4
  191.0 0.2 add.102
  191.2 1.9 collective-permute-start.5
  193.2 1.9 collective-permute-start.2
  195.1 79.7 %collective-permute-done.2 = bf16[512,1152]{1,0:T(8,128)(2,1)S(1)} collective-permute-done((bf16[512,1152]{1,0:T(8,128)(2,1)S(1)}, bf16[512,1152]{1,0:T(8,128)(2,1)S(1)}, u32[]{:S(2)}, u32[]{:S(2)}) %collective-permute-start.2) | collective-permute-done | bytes 1179680 | tf_op jit(solution)/shard_map/ppermute | solution.py:15
  274.8 1.5 fusion.20
  276.3 1.1 fusion.22
  277.4 0.0 collective-permute-done.5
  277.4 0.2 add.103
  277.6 2.1 collective-permute-start.6
  279.7 0.9 fusion.24
  280.7 0.9 convolution_add_fusion.3
  281.6 0.9 convolution_add_fusion.2
  282.5 0.6 add_multiply_fusion
  283.1 1.2 fusion.4
  284.4 1.5 fusion.7
  285.9 145.9 %collective-permute-done.6 = f32[512,1152]{1,0:T(8,128)S(1)} collective-permute-done((f32[512,1152]{1,0:T(8,128)S(1)}, f32[512,1152]{1,0:T(8,128)S(1)}, u32[]{:S(2)}, u32[]{:S(2)}) %collective-permute-start.6) | collective-permute-done | bytes 2359328 | tf_op jit(solution)/shard_map/ppermute | solution.py:15
  431.8 0.5 fusion.8
  432.2 1.5 fusion.11
  (2 shorter events, 0.0 us)
Async XLA Ops:
  0.6 4.9 %copy-start.1 = (bf16[512,1152]{1,0:T(8,128)(2,1)S(1)}, bf16[512,1152]{1,0:T(8,128)(2,1)}, u32[]{:S(2)}) copy-start(bf16[512,1152]{1,0:T(8,128)(2,1)} %param.4) | copy-start | bytes 3538948
  0.6 3.3 copy-start
  8.2 94.6 %collective-permute-start.3 = (f32[512,1152]{1,0:T(8,128)S(1)}, f32[512,1152]{1,0:T(8,128)S(1)}, u32[]{:S(2)}, u32[]{:S(2)}) collective-permute-start(f32[512,1152]{1,0:T(8,128)S(1)} %fusion.23), channel_id=1, source_target_pairs={{0,4},{4,8},{8,12},{12,16},{16,20},{20,24},{24,28},{28,32},{32,36}... | collective-permute-start | bytes 7077896 | tf_op jit(solution)/shard_map/ppermute | solution.py:15
  12.3 89.1 %collective-permute-start = (bf16[512,1152]{1,0:T(8,128)(2,1)S(1)}, bf16[512,1152]{1,0:T(8,128)(2,1)S(1)}, u32[]{:S(2)}, u32[]{:S(2)}) collective-permute-start(bf16[512,1152]{1,0:T(8,128)(2,1)S(1)} %fusion.3), channel_id=1, source_target_pairs={{0,4},{4,8},{8,12},{12,16},{16,20},{20,24},{24,28},{28,32},{32,36}... | collective-permute-start | bytes 3538952 | tf_op jit(solution)/shard_map/ppermute | solution.py:15
  103.9 87.0 %collective-permute-start.4 = (f32[512,1152]{1,0:T(8,128)S(1)}, f32[512,1152]{1,0:T(8,128)S(1)}, u32[]{:S(2)}, u32[]{:S(2)}) collective-permute-start(f32[512,1152]{1,0:T(8,128)S(1)} %convolution_add_fusion), channel_id=1, source_target_pairs={{0,4},{4,8},{8,12},{12,16},{16,20},{20,24},{24,28},{28,32},{32,36}... | collective-permute-start | bytes 7077896 | tf_op jit(solution)/shard_map/ppermute | solution.py:15
  105.9 82.5 %collective-permute-start.1 = (bf16[512,1152]{1,0:T(8,128)(2,1)S(1)}, bf16[512,1152]{1,0:T(8,128)(2,1)S(1)}, u32[]{:S(2)}, u32[]{:S(2)}) collective-permute-start(bf16[512,1152]{1,0:T(8,128)(2,1)S(1)} %collective-permute-done), channel_id=1, source_target_pairs={{0,4},{4,8},{8,12},{12,16},{16,20},{20,24},{24,28},{28,32},{32,36}... | collective-permute-start | bytes 3538952 | tf_op jit(solution)/shard_map/ppermute | solution.py:15
  191.2 86.1 %collective-permute-start.5 = (f32[512,1152]{1,0:T(8,128)S(1)}, f32[512,1152]{1,0:T(8,128)S(1)}, u32[]{:S(2)}, u32[]{:S(2)}) collective-permute-start(f32[512,1152]{1,0:T(8,128)S(1)} %add.102), channel_id=1, source_target_pairs={{0,4},{4,8},{8,12},{12,16},{16,20},{20,24},{24,28},{28,32},{32,36}... | collective-permute-start | bytes 7077896 | tf_op jit(solution)/shard_map/ppermute | solution.py:15
  193.2 81.6 %collective-permute-start.2 = (bf16[512,1152]{1,0:T(8,128)(2,1)S(1)}, bf16[512,1152]{1,0:T(8,128)(2,1)S(1)}, u32[]{:S(2)}, u32[]{:S(2)}) collective-permute-start(bf16[512,1152]{1,0:T(8,128)(2,1)S(1)} %collective-permute-done.1), channel_id=1, source_target_pairs={{0,4},{4,8},{8,12},{12,16},{16,20},{20,24},{24,28},{28,32},{32,36}... | collective-permute-start | bytes 3538952 | tf_op jit(solution)/shard_map/ppermute | solution.py:15
  277.6 154.1 %collective-permute-start.6 = (f32[512,1152]{1,0:T(8,128)S(1)}, f32[512,1152]{1,0:T(8,128)S(1)}, u32[]{:S(2)}, u32[]{:S(2)}) collective-permute-start(f32[512,1152]{1,0:T(8,128)S(1)} %add.103), channel_id=1, source_target_pairs={{0,500},{4,504},{8,508},{12,0},{16,4},{20,8},{24,12},{28,16},{32,2... | collective-permute-start | bytes 7077896 | tf_op jit(solution)/shard_map/ppermute | solution.py:15
where the time goes:
time: 435 us; the launch traced here: 434 us
  waiting for transfers between devices  392 us (90%)
  starting transfers between devices  17 us (4%)
  matrix products  14.5 us (3%)
  other arithmetic  8.13 us (2%)
    ppermute x7, waiting for transfers between devices, shifted(): return lax.ppermute(value, axis, pairs)  392 us
    ppermute x7, starting transfers between devices, shifted(): return lax.ppermute(value, axis, pairs)  17 us
  transfers between devices with their start and end apart: 7, of which 4 were waited for; matrix products, arithmetic and copies ran while one was open for 3% of the time, Pallas kernels for 0%

commit v1 on v0

v1 whole, which is shorter than its diff:
```python
import functools

import jax
import jax.numpy as jnp
from jax import lax
from jax.experimental import pallas as pl
from jax.experimental.pallas import tpu as pltpu
from jax.sharding import PartitionSpec as P

STEPS = 4
EPS = 1e-06
CHUNK = 128
LANES = 128
MESH = pl.DeviceIdType.MESH


def unit_rows(raw):
    widened = raw.astype(jnp.float32)
    inverse = lax.rsqrt(jnp.sum(widened * widened, axis=-1, keepdims=True) + EPS)
    return (widened * inverse).astype(jnp.bfloat16), inverse


def kernel(cycle, scale_ref, bias_ref, img_hbm, txt_hbm, igrad_ref, tgrad_ref, loss_ref,
           raw, held, inverse, total, along, losses, in_sem, send_sem, recv_sem):
    rows, width = img_hbm.shape
    chunks = rows // CHUNK
    me = lax.axis_index("dp")
    group = lax.axis_index("group")
    after = (lax.rem(me + 1, cycle), group)
    before = (lax.rem(me + cycle - 1, cycle), group)
    targets = (before, after)
    embeds = (img_hbm, txt_hbm)
    grads = (igrad_ref, tgrad_ref)

    def piece(chunk):
        return pl.ds(pl.multiple_of(chunk * CHUNK, CHUNK), CHUNK)

    def load(side, chunk):
        return pltpu.make_async_copy(
            embeds[side].at[piece(chunk)], raw.at[side, piece(chunk)], in_sem.at[side, chunk]
        )

    def hop(side, slot, chunk):
        return pltpu.make_async_remote_copy(
            src_ref=held.at[side, slot, piece(chunk)],
            dst_ref=held.at[side, slot + 1, piece(chunk)],
            send_sem=send_sem.at[side, slot, chunk],
            recv_sem=recv_sem.at[side, slot, chunk],
            device_id=targets[side],
            device_id_type=MESH,
        )

    for chunk in range(chunks):
        for side in range(2):
            load(side, chunk).start()

    barrier = pltpu.get_barrier_semaphore()
    for neighbour in targets:
        pl.semaphore_signal(barrier, inc=1, device_id=neighbour, device_id_type=MESH)

    for chunk in range(chunks):
        for side in range(2):
            load(side, chunk).wait()
            normed, scaled = unit_rows(raw[side, piece(chunk)])
            held[side, 0, piece(chunk)] = normed
            inverse[side, piece(chunk)] = jnp.broadcast_to(scaled, (CHUNK, LANES))
            if chunk == 0 and side == 0:
                pl.semaphore_wait(barrier, 2)
            hop(side, 0, chunk).start()

    scale = scale_ref[0]
    bias = bias_ref[0]
    total[...] = jnp.zeros_like(total)
    along[...] = jnp.zeros_like(along)
    losses[...] = jnp.zeros_like(losses)
    row_index = lax.broadcasted_iota(jnp.int32, (rows, CHUNK), 0)
    column_index = lax.broadcasted_iota(jnp.int32, (rows, CHUNK), 1)

    def step(index, carry):
        slot = index // chunks
        chunk = lax.rem(index, chunks)

        @pl.when(slot > 0)
        def _():
            for side in range(2):
                hop(side, slot - 1, chunk).wait_recv()

                @pl.when(slot < STEPS - 1)
                def _():
                    hop(side, slot, chunk).start()

        positive = column_index + jnp.where(slot == 0, chunk * CHUNK, -rows) == row_index
        for side in range(2):
            own = held[side, 0]
            other = held[1 - side, slot, piece(chunk)]
            similar = lax.dot_general(
                own, other, (((1,), (1,)), ((), ())), preferred_element_type=jnp.float32
            )
            logits = scale * similar + bias
            signed = jnp.where(positive, -logits, logits)
            small = jnp.exp(-jnp.abs(signed))
            share = pl.reciprocal(1.0 + small)
            sigmoid = jnp.where(signed >= 0, share, small * share)
            weights = (scale * jnp.where(positive, -sigmoid, sigmoid)).astype(jnp.bfloat16)
            if side == 0:
                series = small * (1.0 - small * (0.5 - small * (1.0 / 3.0)))
                tail = jnp.where(small < 0.0078125, series, jnp.log(1.0 + small))
                losses[...] += jnp.maximum(signed, 0.0) + tail
            along[side] += weights.astype(jnp.float32) * similar
            total[side] += jnp.dot(weights, other, preferred_element_type=jnp.float32)
        return carry

    lax.fori_loop(0, STEPS * chunks, step, 0)

    for chunk in range(chunks):
        for side in range(2):
            part = piece(chunk)
            dot_sum = jnp.sum(along[side, part], axis=-1, keepdims=True)
            widened = held[side, 0, part].astype(jnp.float32)
            grads[side][part] = (
                (total[side, part] - widened * dot_sum) * inverse[side, part, 0:1]
            ).astype(jnp.bfloat16)
    loss_ref[...] = jnp.sum(losses[...].T, axis=0, keepdims=True) * (1.0 / (STEPS * rows))

    for chunk in range(chunks):
        for side in range(2):
            for slot in range(STEPS - 1):
                hop(side, slot, chunk).wait_send()


def local(image_embeds, text_embeds, logit_scale, logit_bias):
    rows, width = image_embeds.shape
    chunks = rows // CHUNK
    dma = pltpu.SemaphoreType.DMA
    image_grad, text_grad, loss = pl.pallas_call(
        functools.partial(kernel, lax.axis_size("dp")),
        out_shape=(
            jax.ShapeDtypeStruct((rows, width), jnp.bfloat16),
            jax.ShapeDtypeStruct((rows, width), jnp.bfloat16),
            jax.ShapeDtypeStruct((1, rows), jnp.float32),
        ),
        in_specs=[
            pl.BlockSpec(memory_space=pltpu.SMEM),
            pl.BlockSpec(memory_space=pltpu.SMEM),
            pl.BlockSpec(memory_space=pltpu.HBM),
            pl.BlockSpec(memory_space=pltpu.HBM),
        ],
        out_specs=(
            pl.BlockSpec(memory_space=pltpu.VMEM),
            pl.BlockSpec(memory_space=pltpu.VMEM),
            pl.BlockSpec(memory_space=pltpu.VMEM),
        ),
        scratch_shapes=[
            pltpu.VMEM((2, rows, width), jnp.bfloat16),
            pltpu.VMEM((2, STEPS, rows, width), jnp.bfloat16),
            pltpu.VMEM((2, rows, LANES), jnp.float32),
            pltpu.VMEM((2, rows, width), jnp.float32),
            pltpu.VMEM((2, rows, CHUNK), jnp.float32),
            pltpu.VMEM((rows, CHUNK), jnp.float32),
            dma((2, chunks)),
            dma((2, STEPS - 1, chunks)),
            dma((2, STEPS - 1, chunks)),
        ],
        compiler_params=pltpu.CompilerParams(
            collective_id=0, has_side_effects=True, vmem_limit_bytes=48 * 2**20
        ),
        cost_estimate=pl.CostEstimate(
            flops=32 * rows * rows * width, bytes_accessed=8 * rows * width, transcendentals=24 * rows * rows
        ),
        name="band_loss",
    )(logit_scale, logit_bias, image_embeds, text_embeds)
    return image_grad, text_grad, loss.reshape(rows)


def solution(mesh):
    in_specs = (P(("group", "dp"), None), P(("group", "dp"), None), P(), P())
    out_specs = (P(("group", "dp"), None), P(("group", "dp"), None), P(("group", "dp")))
    return jax.shard_map(local, mesh=mesh, in_specs=in_specs, out_specs=out_specs, check_vma=False)
```

time: 435 us -> 104 us (0.24)
  waiting for transfers between devices: 392 us -> 0 us
  Pallas kernels: 0 us -> 96.9 us
  starting transfers between devices: 17 us -> 0 us
  matrix products: 14.5 us -> 0 us
  other arithmetic: 8.13 us -> 0 us
  local copies, waits for them, and re-layouts: 0.01 us -> 5.14 us
    ppermute x7 -> x0, waiting for transfers between devices: 392 us -> none  [shifted(): return lax.ppermute(value, axis, pairs)]
    pallas_call x0 -> x1, Pallas kernels: none -> 96.9 us  [local(): pl.pallas_call(functools.partial(kernel, lax.axis_size('dp')), out_shape=...]
    ppermute x7 -> x0, starting transfers between devices: 17 us -> none  [shifted(): return lax.ppermute(value, axis, pairs)]
    dot_general x12 -> x0, matrix products: 14.5 us -> none  [the longest x4 6.05 us: local(): lax.dot_general(img_norm, text_block, (((1,), (1,)), ((), ())), preferred...]
    unnamed x4 -> x7, local copies, waits for them, and re-layouts: 0.01 us -> 5.14 us
  transfers between devices with their start and end apart: 7 -> 0, of which waited for: 4 -> 0; matrix products, arithmetic and copies ran while one was open for 3% -> 0% of each run, Pallas kernels for 0% -> 0%
where the time goes in v1:
time: 104 us
  Pallas kernels  96.9 us (93%)
  local copies, waits for them, and re-layouts  5.14 us (5%)
  between operations  1.94 us (2%)
    pallas_call x1, Pallas kernels, local(): pl.pallas_call(functools.partial(kernel, lax.axis_size('dp')), out_shape=...  96.9 us
    unnamed x7, local copies, waits for them, and re-layouts  5.14 us

profile of v1, /device:TPU:1, one launch (start us, length us, event | category | flops | bytes accessed | tf_op | source)
XLA Modules:
  0.0 104.0 jit_solution(18010932990754014765)
XLA Ops:
  1.9 0.0 copy-start
  1.9 1.3 %copy-done = bf16[512,1152]{1,0:T(8,128)(2,1)S(1)} copy-done((bf16[512,1152]{1,0:T(8,128)(2,1)S(1)}, bf16[512,1152]{1,0:T(8,128)(2,1)}, u32[]{:S(2)}) %copy-start) | copy-done | bytes 1179672
  3.2 0.0 copy-start.1
  3.2 1.3 %copy-done.1 = bf16[512,1152]{1,0:T(8,128)(2,1)S(1)} copy-done((bf16[512,1152]{1,0:T(8,128)(2,1)S(1)}, bf16[512,1152]{1,0:T(8,128)(2,1)}, u32[]{:S(2)}) %copy-start.1) | copy-done | bytes 1179672
  4.5 96.9 %band_loss.1 = (bf16[512,1152]{1,0:T(8,128)(2,1)S(1)}, bf16[512,1152]{1,0:T(8,128)(2,1)S(1)}, f32[1,512]{1,0:T(1,128)S(1)}) custom-call(f32[1]{0:T(128)S(6)} %copy.10.scale_ref, f32[1]{0:T(128)S(6)} %copy.11.bias_ref, bf16[512,1152]{1,0:T(8,128)(2,1)S(1)} %copy-done, bf16[512,1152]{1,0:T(8,128)(2,1)S(1)} %copy-done.1), custom_call_target="tpu_custom_call" | custom-call | flops 9663676416 | bytes 4718592 | tf_op jit(solution)/shard_map/band_loss/pallas_call | solution.py:135
  101.4 1.0 copy.12
  102.4 1.0 copy.13
  103.4 0.6 copy.14
Async XLA Ops:
  1.9 1.3 %copy-start = (bf16[512,1152]{1,0:T(8,128)(2,1)S(1)}, bf16[512,1152]{1,0:T(8,128)(2,1)}, u32[]{:S(2)}) copy-start(bf16[512,1152]{1,0:T(8,128)(2,1)} %img_hbm.1) | copy-start | bytes 3538948
  3.2 1.3 %copy-start.1 = (bf16[512,1152]{1,0:T(8,128)(2,1)S(1)}, bf16[512,1152]{1,0:T(8,128)(2,1)}, u32[]{:S(2)}) copy-start(bf16[512,1152]{1,0:T(8,128)(2,1)} %txt_hbm.1) | copy-start | bytes 3538948

commit v2 on v1

v2 whole, which is shorter than its diff:
```python
import functools

import jax
import jax.numpy as jnp
from jax import lax
from jax.experimental import pallas as pl
from jax.experimental.pallas import tpu as pltpu
from jax.sharding import PartitionSpec as P

STEPS = 4
EPS = 1e-06
CHUNK = 128
LANES = 128
LINE = 8
SEATS = 64
DETOURS = (((0, 0, 64), (0, 64, 48), (1, 0, 32)), ((0, 0, 64), (0, 64, 64), (1, 0, 48)))
RELAY_STEP = (3, 2)
DETOUR_CHUNKS = tuple(1 + max(piece[0] for piece in pieces) for pieces in DETOURS)
RELAY_ROWS = 64
MESH = pl.DeviceIdType.MESH


def unit_rows(raw):
    widened = raw.astype(jnp.float32)
    inverse = lax.rsqrt(jnp.sum(widened * widened, axis=-1, keepdims=True) + EPS)
    return (widened * inverse).astype(jnp.bfloat16), inverse


def chunk_rows(chunk):
    return pl.ds(pl.multiple_of(chunk * CHUNK, CHUNK), CHUNK)


def band_kernel(cycle, scale_ref, bias_ref, img_hbm, txt_hbm, own, inverse, total, along, losses, final, final_weights,
                raw, held, relay, in_sem, send_sem, recv_sem, relay_send, relay_recv, late_sem):
    rows, width = img_hbm.shape
    chunks = rows // CHUNK
    last = chunks - 1
    me = lax.axis_index("dp")
    group = lax.axis_index("group")
    seat = lax.rem(me, SEATS)

    def device(shift):
        return (lax.rem(me + shift + cycle, cycle), group)

    targets = (device(-1), device(1))
    embeds = (img_hbm, txt_hbm)
    first, end = seat == 0, seat == SEATS - 1
    relays = len(DETOURS[0])
    text_relay = (lax.rem(seat, LINE) == LINE - 1) & (seat < relays * LINE)
    image_relay = (lax.rem(seat, LINE) == 0) & (seat >= SEATS - relays * LINE)

    second, before_end = seat == 1, seat == SEATS - 2

    def chunk_at(side, slot, place):
        if side:
            late = (first & (slot == 1)) | (second & (slot == 2))
        else:
            late = (end & (slot == 1)) | (before_end & (slot == 2))
        return lax.rem(place + jnp.where(late, DETOUR_CHUNKS[side], 0), chunks)

    def away(place):
        return (place + 1) * LINE

    def load(side, chunk):
        return pltpu.make_async_copy(
            embeds[side].at[chunk_rows(chunk)], raw.at[side, chunk_rows(chunk)], in_sem.at[side, chunk]
        )

    def remote(source, target, done, arrived, to):
        return pltpu.make_async_remote_copy(
            src_ref=source, dst_ref=target, send_sem=done, recv_sem=arrived, device_id=to, device_id_type=MESH
        )

    def hop(side, slot, chunk, part=None, first=False):
        source = max(slot - 1, 0) if isinstance(slot, int) else jnp.maximum(slot - 1, 0)
        block = own.at[side] if first else held.at[side, source]
        span = chunk_rows(chunk) if part is None else pl.ds(chunk * CHUNK + part[0], part[1])
        return remote(
            block.at[span], held.at[side, slot, span], send_sem.at[side, slot, chunk], recv_sem.at[side, slot, chunk],
            targets[side],
        )

    def to_relay(side, place):
        chunk, start, length = DETOURS[side][place]
        return remote(
            held.at[side, 0, pl.ds(chunk * CHUNK + start, length)], relay.at[pl.ds(0, length)],
            send_sem.at[side, 1, chunk], relay_recv, device(away(place) if side else -away(place)),
        )

    def from_relay(side, place):
        chunk, start, length = DETOURS[side][place]
        return remote(
            relay.at[pl.ds(0, length)], held.at[side, 1, pl.ds(chunk * CHUNK + start, length)], relay_send,
            recv_sem.at[side, 1, chunk], device(1 - away(place) if side else away(place) - 1),
        )

    def send_by_relays(side, chunk):
        sent = sum(piece[2] for piece in DETOURS[side] if piece[0] == chunk)
        if sent < CHUNK:
            hop(side, 1, chunk, (sent, CHUNK - sent)).start()
        for place, piece in enumerate(DETOURS[side]):
            if piece[0] == chunk:
                to_relay(side, place).start()

    def relay_seat(side, place):
        return seat == (away(place) - 1 if side else SEATS - away(place))

    for chunk in range(chunks):
        for side in (1, 0):
            load(side, chunk).start()

    barrier = pltpu.get_barrier_semaphore()

    def greet(shift):
        pl.semaphore_signal(barrier, inc=1, device_id=device(shift), device_id_type=MESH)

    greet(-1)

    @pl.when(jnp.logical_not(end))
    def _():
        greet(1)

    @pl.when(first)
    def _():
        for place in range(relays):
            greet(away(place) - 1)
            greet(-away(place))

    @pl.when(text_relay)
    def _():
        greet(-1 - seat)

    @pl.when(end)
    def _():
        for place in range(relays):
            greet(1 - away(place))

    one = lambda flag, count: jnp.where(flag, count, 0)
    expected = 2 - one(first, 1) + one(text_relay, 1) + one(image_relay, 2)

    @pl.when(end)
    def _():
        pl.semaphore_wait(barrier, 2 + relays)
        pl.semaphore_signal(late_sem.at[0], inc=1, device_id=device(1), device_id_type=MESH)

    for chunk in range(chunks):
        for side in (1, 0):
            load(side, chunk).wait()
            normed, scaled = unit_rows(raw[side, chunk_rows(chunk)])
            own[side, chunk_rows(chunk)] = normed
            inverse[side, chunk_rows(chunk)] = jnp.broadcast_to(scaled, (CHUNK, LANES))
            if chunk == 0 and side == 1:
                @pl.when(jnp.logical_not(end))
                def _():
                    pl.semaphore_wait(barrier, expected)

                @pl.when(image_relay)
                def _():
                    pl.semaphore_signal(late_sem.at[1], inc=1, device_id=device(SEATS - seat), device_id_type=MESH)

            if side == 0:

                @pl.when(jnp.logical_not(first))
                def _():
                    hop(0, 0, chunk, first=True).start()

            else:
                hop(1, 0, chunk, first=True).start()

    scale = scale_ref[...].reshape(1, 1)
    bias = bias_ref[...].reshape(1, 1)
    row_index = lax.broadcasted_iota(jnp.int32, (rows, CHUNK), 0)
    column_index = lax.broadcasted_iota(jnp.int32, (rows, CHUNK), 1)

    def slopes(side, other, positive):
        similar = lax.dot_general(
            own[side], other, (((1,), (1,)), ((), ())), preferred_element_type=jnp.float32
        )
        logits = scale * similar + bias
        signed = logits if positive is None else jnp.where(positive, -logits, logits)
        small = jnp.exp(-jnp.abs(signed))
        share = pl.reciprocal(1.0 + small)
        sigmoid = jnp.where(signed >= 0, share, small * share)
        slope = sigmoid if positive is None else jnp.where(positive, -sigmoid, sigmoid)
        weights = (scale * slope).astype(jnp.bfloat16)
        if side == 0:
            series = small * (1.0 - small * (0.5 - small * (1.0 / 3.0)))
            rest = jnp.where(small < 0.0078125, series, jnp.log(1.0 + small))
            losses[...] += jnp.maximum(signed, 0.0) + rest
        along[side] += weights.astype(jnp.float32) * similar
        return weights

    def pairs(side, other, positive):
        weights = slopes(side, other, positive)
        total[side] += jnp.dot(weights, other, preferred_element_type=jnp.float32)

    total[...] = jnp.zeros_like(total)
    along[...] = jnp.zeros_like(along)
    losses[...] = jnp.zeros_like(losses)

    def own_step(chunk, carry):
        positive = column_index + chunk * CHUNK == row_index
        for side in range(2):
            pairs(side, own[1 - side, chunk_rows(chunk)], positive)
        return carry

    lax.fori_loop(0, chunks, own_step, 0)

    @pl.when(first)
    def _():
        pl.semaphore_wait(late_sem.at[0], 1)
        pl.semaphore_wait(late_sem.at[1], relays)
        for chunk in range(chunks):
            hop(0, 0, chunk, first=True).start()

    def step(index, carry):
        slot = index // chunks
        taken = [chunk_at(side, slot, lax.rem(index, chunks)) for side in range(2)]
        for side in (1, 0):
            hop(side, slot, taken[side]).wait_recv()
            by_relay = (end if side else first) & (index < DETOUR_CHUNKS[side])

            @pl.when((slot < STEPS - 2) & jnp.logical_not(by_relay))
            def _():
                hop(side, slot + 1, taken[side]).start()

            for chunk in range(DETOUR_CHUNKS[side]):

                @pl.when(by_relay & (index == chunk))
                def _():
                    send_by_relays(side, chunk)

        for side in range(2):
            pairs(side, held[1 - side, slot, chunk_rows(taken[1 - side])], None)

        for side in range(2):
            for place in range(relays):

                @pl.when(relay_seat(side, place) & (index == DETOURS[side][place][0] + RELAY_STEP[side]))
                def _():
                    to_relay(side, place).wait_recv()
                    from_relay(side, place).start()

        return carry

    lax.fori_loop(0, (STEPS - 1) * chunks - 1, step, 0)

    taken = [chunk_at(side, STEPS - 2, last) for side in range(2)]
    for side in range(2):
        hop(side, STEPS - 2, taken[side]).wait_recv()
    for side in range(2):
        other = held[1 - side, STEPS - 2, chunk_rows(taken[1 - side])]
        final[side] = other
        final_weights[side] = slopes(side, other, None)

    for slot in range(STEPS - 1):
        for chunk in range(chunks):
            for side in range(2):
                hop(side, slot, chunk, first=slot == 0).wait_send()

    for side in range(2):
        for place in range(relays):

            @pl.when(relay_seat(side, place))
            def _():
                from_relay(side, place).wait_send()


def finish_kernel(own, inverse, total, along, losses, final, final_weights, igrad_hbm, tgrad_hbm, loss_hbm,
                  outs, loss, out_sem, loss_sem):
    rows, width = own.shape[1:]
    grads = (igrad_hbm, tgrad_hbm)
    loss[...] = jnp.sum(losses[...].T, axis=0, keepdims=True) * (1.0 / (STEPS * rows))
    copies = [pltpu.make_async_copy(loss, loss_hbm, loss_sem)]
    copies[0].start()
    for chunk in range(rows // CHUNK):
        for side in range(2):
            part = chunk_rows(chunk)
            dot_sum = jnp.sum(along[side, part], axis=-1, keepdims=True)
            widened = own[side, part].astype(jnp.float32)
            rest = jnp.dot(final_weights[side, part], final[side], preferred_element_type=jnp.float32)
            outs[side, part] = (
                (total[side, part] + rest - widened * dot_sum) * inverse[side, part, 0:1]
            ).astype(jnp.bfloat16)
            copy = pltpu.make_async_copy(outs.at[side, part], grads[side].at[part], out_sem.at[side, chunk])
            copy.start()
            copies.append(copy)
    for copy in copies:
        copy.wait()


def local(image_embeds, text_embeds, logit_scale, logit_bias):
    rows, width = image_embeds.shape
    chunks = rows // CHUNK
    hops = STEPS - 1
    dma = pltpu.SemaphoreType.DMA
    vmem = pl.BlockSpec(memory_space=pltpu.VMEM)
    hbm = pl.BlockSpec(memory_space=pl.ANY)
    sums = pl.pallas_call(
        functools.partial(band_kernel, lax.axis_size("dp")),
        out_shape=(
            jax.ShapeDtypeStruct((2, rows, width), jnp.bfloat16),
            jax.ShapeDtypeStruct((2, rows, LANES), jnp.float32),
            jax.ShapeDtypeStruct((2, rows, width), jnp.float32),
            jax.ShapeDtypeStruct((2, rows, CHUNK), jnp.float32),
            jax.ShapeDtypeStruct((rows, CHUNK), jnp.float32),
            jax.ShapeDtypeStruct((2, CHUNK, width), jnp.bfloat16),
            jax.ShapeDtypeStruct((2, rows, CHUNK), jnp.bfloat16),
        ),
        in_specs=[vmem, vmem, hbm, hbm],
        out_specs=(vmem,) * 7,
        scratch_shapes=[
            pltpu.VMEM((2, rows, width), jnp.bfloat16),
            pltpu.VMEM((2, hops, rows, width), jnp.bfloat16),
            pltpu.VMEM((RELAY_ROWS, width), jnp.bfloat16),
            dma((2, chunks)),
            dma((2, hops, chunks)),
            dma((2, hops, chunks)),
            dma,
            dma,
            pltpu.SemaphoreType.REGULAR((2,)),
        ],
        compiler_params=pltpu.CompilerParams(
            collective_id=0, has_side_effects=True, vmem_limit_bytes=36 * 2**20
        ),
        cost_estimate=pl.CostEstimate(
            flops=32 * rows * rows * width, bytes_accessed=8 * rows * width, transcendentals=24 * rows * rows
        ),
        name="band_sums",
    )(
        logit_scale,
        logit_bias,
        *(pltpu.with_memory_space_constraint(array, pltpu.HBM) for array in (image_embeds, text_embeds)),
    )
    image_grad, text_grad, loss = pl.pallas_call(
        finish_kernel,
        out_shape=(
            jax.ShapeDtypeStruct((rows, width), jnp.bfloat16),
            jax.ShapeDtypeStruct((rows, width), jnp.bfloat16),
            jax.ShapeDtypeStruct((1, rows), jnp.float32),
        ),
        in_specs=[vmem] * 7,
        out_specs=(hbm,) * 3,
        scratch_shapes=[
            pltpu.VMEM((2, rows, width), jnp.bfloat16),
            pltpu.VMEM((1, rows), jnp.float32),
            dma((2, chunks)),
            dma,
        ],
        compiler_params=pltpu.CompilerParams(vmem_limit_bytes=36 * 2**20),
        cost_estimate=pl.CostEstimate(flops=8 * rows * width, bytes_accessed=16 * rows * width, transcendentals=0),
        name="finish",
    )(*sums)
    return image_grad, text_grad, loss.reshape(rows)


def solution(mesh):
    in_specs = (P(("group", "dp"), None), P(("group", "dp"), None), P(), P())
    out_specs = (P(("group", "dp"), None), P(("group", "dp"), None), P(("group", "dp")))
    return jax.shard_map(local, mesh=mesh, in_specs=in_specs, out_specs=out_specs, check_vma=False)
```

time: 104 us -> 90.4 us (0.87)
  Pallas kernels: 96.9 us -> 88.2 us
  local copies, waits for them, and re-layouts: 5.14 us -> 0 us
    pallas_call x1 -> x2, Pallas kernels: 96.9 us -> 88.2 us  [the longest x1 86.1 us: local(): pl.pallas_call(functools.partial(band_kernel, lax.axis_size('dp')), out_s...]
    unnamed x7 -> x0, local copies, waits for them, and re-layouts: 5.14 us -> none
where the time goes in v2:
time: 90.4 us; the launch traced here: 90.1 us
  Pallas kernels  88.2 us (98%)
  between operations  1.93 us (2%)
    pallas_call x1, Pallas kernels, local(): pl.pallas_call(functools.partial(band_kernel, lax.axis_size('dp')), out_s...  86.1 us
    pallas_call x1, Pallas kernels, local(): pl.pallas_call(finish_kernel, out_shape=(jax.ShapeDtypeStruct((rows, widt...  2.11 us

profile of v2, /device:TPU:1, one launch (start us, length us, event | category | flops | bytes accessed | tf_op | source)
XLA Modules:
  0.0 90.1 jit_solution(7464015180875844567)
XLA Ops:
  1.9 86.1 %band_sums.1 = (bf16[2,512,1152]{2,1,0:T(8,128)(2,1)S(1)}, f32[2,512,128]{2,1,0:T(8,128)S(1)}, f32[2,512,1152]{2,1,0:T(8,128)S(1)}, f32[2,512,128]{2,1,0:T(8,128...) custom-call(f32[1]{0:T(128)S(6)} %copy.7.scale_ref, ...), custom_call_target="tpu_custom_call" | custom-call | flops 9663676416 | bytes 4718592 | tf_op jit(solution)/shard_map/band_sums/pallas_call | solution.py:299
  88.0 2.1 %finish.1 = (bf16[512,1152]{1,0:T(8,128)(2,1)}, bf16[512,1152]{1,0:T(8,128)(2,1)}, f32[1,512]{1,0:T(1,128)}) custom-call(bf16[2,512,1152]{2,1,0:T(8,128)(2,1)S(1)} %get-tuple-element.13.own, f32[2,512,128]{2,1,0:T(8,128)S(1)} %get-tuple-element.14.inverse, f32[2,512,1152]{2,1,0:T(8,128)S(1)} %get-tuple-element.15.total, ...), custom_call_target="tpu_custom_call" | custom-call | flops 4718592 | bytes 9437184 | tf_op jit(solution)/shard_map/finish/pallas_call | solution.py:335

commit v3 on v2

--- a/solution.py
+++ b/solution.py
@@ -245,6 +245,18 @@
 
     lax.fori_loop(0, (STEPS - 1) * chunks - 1, step, 0)
 
+    for slot in range(STEPS - 2):
+        for chunk in range(chunks):
+            for side in range(2):
+                hop(side, slot, chunk, first=slot == 0).wait_send()
+
+    for side in range(2):
+        for place in range(relays):
+
+            @pl.when(relay_seat(side, place))
+            def _():
+                from_relay(side, place).wait_send()
+
     taken = [chunk_at(side, STEPS - 2, last) for side in range(2)]
     for side in range(2):
         hop(side, STEPS - 2, taken[side]).wait_recv()
@@ -253,17 +265,9 @@
         final[side] = other
         final_weights[side] = slopes(side, other, None)
 
-    for slot in range(STEPS - 1):
-        for chunk in range(chunks):
-            for side in range(2):
-                hop(side, slot, chunk, first=slot == 0).wait_send()
-
-    for side in range(2):
-        for place in range(relays):
-
-            @pl.when(relay_seat(side, place))
-            def _():
-                from_relay(side, place).wait_send()
+    for chunk in range(chunks):
+        for side in range(2):
+            hop(side, STEPS - 2, chunk).wait_send()
 
 
 def finish_kernel(own, inverse, total, along, losses, final, final_weights, igrad_hbm, tgrad_hbm, loss_hbm,

time: 90.4 us -> 90.4 us (level)
  no operation moved by 1% of the time
where the time goes in v3:
time: 90.4 us; the launch traced here: 90.1 us
  Pallas kernels  88.2 us (98%)
  between operations  1.93 us (2%)
    pallas_call x1, Pallas kernels, local(): pl.pallas_call(functools.partial(band_kernel, lax.axis_size('dp')), out_s...  86.1 us
    pallas_call x1, Pallas kernels, local(): pl.pallas_call(finish_kernel, out_shape=(jax.ShapeDtypeStruct((rows, widt...  2.11 us

profile of v3, /device:TPU:1, one launch (start us, length us, event | category | flops | bytes accessed | tf_op | source)
XLA Modules:
  0.0 90.1 jit_solution(18058402364783456365)
XLA Ops:
  1.9 86.1 %band_sums.1 = (bf16[2,512,1152]{2,1,0:T(8,128)(2,1)S(1)}, f32[2,512,128]{2,1,0:T(8,128)S(1)}, f32[2,512,1152]{2,1,0:T(8,128)S(1)}, f32[2,512,128]{2,1,0:T(8,128...) custom-call(f32[1]{0:T(128)S(6)} %copy.7.scale_ref, ...), custom_call_target="tpu_custom_call" | custom-call | flops 9663676416 | bytes 4718592 | tf_op jit(solution)/shard_map/band_sums/pallas_call | solution.py:303
  88.0 2.1 %finish.1 = (bf16[512,1152]{1,0:T(8,128)(2,1)}, bf16[512,1152]{1,0:T(8,128)(2,1)}, f32[1,512]{1,0:T(1,128)}) custom-call(bf16[2,512,1152]{2,1,0:T(8,128)(2,1)S(1)} %get-tuple-element.13.own, f32[2,512,128]{2,1,0:T(8,128)S(1)} %get-tuple-element.14.inverse, f32[2,512,1152]{2,1,0:T(8,128)S(1)} %get-tuple-element.15.total, ...), custom_call_target="tpu_custom_call" | custom-call | flops 4718592 | bytes 9437184 | tf_op jit(solution)/shard_map/finish/pallas_call | solution.py:339
